TPU v7x, 128 devices: a whole 4x4x4 slice. The times are simulated.
128 devices in a mesh: pool: 32 (over x, z, core), blk: 4 (over y).
Axes of the slice: x: 4, y: 4, z: 4, core: 2. Of those that a mesh axis runs over, the one named last changes fastest.
Arguments:
- embeddings: float32 [131072, 1024], P(('pool', 'blk')), may hold values from -6 to 6
- cluster_ids: int32 [131072, 1], P(('pool', 'blk')), may hold values from 0 to 127; in each aligned block of 1024 rows (0 to 1023, 1024 to 2047, ...) at most 16 rows name the same one
Outputs:
- density: float32 [131072], P(('pool', 'blk'))
Inputs may be any that keep to these rules, and one draw needn't show every extreme that they name: `cluster_ids`: within the rows of one device no cluster appears more than 16 times, and some cluster appears exactly 16 times; every cluster appears in some row.
All inputs are finite; a program needn't handle non-finite values.
Results may differ from a plain program's by a relative error of at most 0.0003.
Values may be sent and summed in bfloat16 or wider, within the bound.
A program may use at most 64 MiB of HBM per device.

v0:
```python
import math

import jax
import jax.numpy as jnp
from jax import lax
from jax.sharding import PartitionSpec as P

SOFTMAX_TEMP = 0.02
EPSILON = 1e-06


def normalized_rows(embeddings):
    squares = jnp.sum(embeddings * embeddings, axis=1, keepdims=True)
    return (embeddings * lax.rsqrt(squares + EPSILON)).astype(jnp.bfloat16)


def ranks_within(identity_matrix, clusters):
    count = identity_matrix.shape[0]
    onehot = (identity_matrix[:, None] == jnp.arange(clusters, dtype=jnp.int32)[None, :]).astype(
        jnp.bfloat16
    )
    lower = (jnp.arange(count)[:, None] > jnp.arange(count)[None, :]).astype(jnp.bfloat16)
    before = jnp.dot(lower, onehot, preferred_element_type=jnp.float32)
    return jnp.sum(before * onehot.astype(jnp.float32), axis=1).astype(jnp.int32)


def cluster_density(members, present):
    count = members.shape[0]
    block = math.gcd(count, 1024)
    duplicate_flags = present.astype(jnp.float32)

    def one_block(begin):
        queries = lax.dynamic_slice_in_dim(members, begin, block, 0)
        density_scores = lax.dot_general(
            queries, members, (((1,), (1,)), ((), ())), preferred_element_type=jnp.float32
        )
        keep_weights = jnp.exp(density_scores / SOFTMAX_TEMP) * duplicate_flags[None, :]
        own = begin + jnp.arange(block, dtype=jnp.int32)[:, None]
        other = jnp.arange(count, dtype=jnp.int32)[None, :]
        keep_weights = jnp.where(own == other, jnp.zeros_like(keep_weights), keep_weights)
        return jnp.log(1.0 + jnp.sum(keep_weights, axis=1))

    starts = jnp.arange(count // block, dtype=jnp.int32) * block
    return lax.map(one_block, starts).reshape(count)


def shards(embeddings, cluster_ids):
    n_pool = lax.axis_size("pool")
    n_blk = lax.axis_size("blk")
    devices = n_pool * n_blk
    rows, width = embeddings.shape
    capacity = 2 * rows // devices
    total = devices * capacity
    unit = normalized_rows(embeddings)
    identity_matrix = cluster_ids[:, 0]
    rank = ranks_within(identity_matrix, devices)
    slot = identity_matrix * capacity + rank
    packed = jnp.zeros((total, width), jnp.bfloat16).at[slot].set(unit)
    present = jnp.zeros((total,), jnp.bfloat16).at[slot].set(jnp.ones((rows,), jnp.bfloat16))
    received, duplicate_flags = (
        lax.all_to_all(
            packed.reshape(devices, capacity, width),
            ("pool", "blk"),
            split_axis=0,
            concat_axis=0,
            tiled=True,
        ),
        lax.all_to_all(
            present.reshape(devices, capacity),
            ("pool", "blk"),
            split_axis=0,
            concat_axis=0,
            tiled=True,
        ),
    )
    dens = cluster_density(received.reshape(total, width), duplicate_flags.reshape(total))
    back = lax.all_to_all(
        dens.reshape(devices, capacity), ("pool", "blk"), split_axis=0, concat_axis=0, tiled=True
    )
    return back.reshape(total)[slot]


def solution(mesh):
    placed = (P(("pool", "blk"), None), P(("pool", "blk"), None))
    return jax.shard_map(
        shards, mesh=mesh, in_specs=placed, out_specs=P(("pool", "blk")), check_vma=False
    )
```

profile of v0, /device:TPU:1, one launch (start us, length us, event | category | flops | bytes accessed | tf_op | source)
XLA Modules:
  0.0 146.7 jit_solution(4287030754912309444)
XLA Ops:
  0.0 1.4 fusion.7
  1.4 0.7 compare_select_fusion
  2.1 7.6 %scatter_custom_fusion.1 = bf16[2048]{0:T(1024)(128)(2,1)S(1)} fusion(s32[1024]{0:T(1024)S(1)} %bitcast.17, bf16[1024]{0:T(1024)(128)(2,1)S(1)} %broadcast.45, bf16[]{:T(256)} %constant.7.clone.1), kind=kCustom, calls=%fused_computation.25 | custom fusion | bytes 4098 | tf_op jit(solution)/shard_map/scatter | solution.py:59
  9.7 0.7 all_to_all.20
  10.4 11.5 %all-to-all-start.1 = ((bf16[128,1,16]{2,1,0:T(2,128)(2,1)}), bf16[128,1,16]{2,1,0:T(2,128)(2,1)S(1)}, u32[]{:S(2)}, u32[]{:S(2)}) async-start(bf16[128,1,16]{2,1,0:T(2,128)(2,1)} %all_to_all.20), calls=%async_computation.1 | async-start | bytes 131072 | tf_op jit(solution)/shard_map/all_to_all | solution.py:68
  21.9 2.5 %multiply_reduce_fusion = f32[1024]{0:T(1024)S(1)} fusion(f32[1024,1024]{1,0:T(8,128)} %param.4), kind=kLoop, calls=%fused_computation.10 | loop fusion | flops 2096128 | bytes 4198400 | tf_op jit(solution)/shard_map/reduce_sum | solution.py:13
  24.5 9.3 %scatter_custom_fusion = bf16[2048,1024]{1,0:T(8,128)(2,1)} fusion(s32[1024]{0:T(1024)S(1)} %bitcast.18, f32[1024,1024]{1,0:T(8,128)} %param.4, f32[1024]{0:T(1024)S(1)} %add_rsqrt_fusion, bf16[]{:T(256)} %constant.7.clone.1), kind=kCustom, calls=%fused_computation.13 | custom fusion | flops 2097152 | bytes 8392706 | tf_op jit(solution)/shard_map/scatter | solution.py:58
  33.7 0.0 all-to-all-done.1
  33.7 10.2 %all-to-all-start = ((bf16[128,16,1024]{2,1,0:T(8,128)(2,1)}), bf16[128,16,1024]{2,1,0:T(8,128)(2,1)}, u32[]{:S(2)}, u32[]{:S(2)}) async-start(bf16[128,16,1024]{2,1,0:T(8,128)(2,1)} %bitcast.15), calls=%async_computation | async-start | bytes 8388608 | tf_op jit(solution)/shard_map/all_to_all | solution.py:61
  44.0 0.2 convert_reduce_fusion
  44.2 0.1 reshape.57
  44.3 52.8 %all-to-all-done = bf16[128,16,1024]{2,1,0:T(8,128)(2,1)} async-done(((bf16[128,16,1024]{2,1,0:T(8,128)(2,1)}), bf16[128,16,1024]{2,1,0:T(8,128)(2,1)}, u32[]{:S(2)}, u32[]{:S(2)}) %all-to-all-start) | async-done | bytes 4194336 | tf_op jit(solution)/shard_map/all_to_all | solution.py:61
  97.1 22.6 %while.10 = (s32[]{:T(128)}, f32[2,1024]{1,0:T(2,128)S(1)}, s32[2]{0:T(128)S(1)}, bf16[2048,1024]{1,0:T(8,128)(2,1)}, f32[2048]{0:T(1024)S(1)}, /*index=5*/s32[]{:T(128)}, s32[]{:T(128)}, s32[]{:T(128)}) while((s32[]{:T(128)}, f32[2,1024]{1,0:T(2,128)S(1)}, s32[2]{0:T(128)S(1)}, bf16[2048,1024]{1,0:T(8,128)(2,1)}, f32[2048]{0:T(1024)S(1)}, ...), condition=%wide.region_6.7_spmd, body=%wide.region_4.6_spmd.sunk | while | flops 4305454080 | bytes 6328463 | solution.py:44
  97.1 0.6 dynamic_slice.12
  99.5 0.6 iota_add_fusion.2
  100.2 8.1 %select_reduce_fusion.2 = f32[1024]{0:T(1024)S(1)} fusion(bf16[2048,1024]{1,0:T(8,128)(2,1)} %get-tuple-element.93, f32[2048]{0:T(1024)S(1)} %get-tuple-element.94, s32[1024]{0:T(1024)S(1)} %iota_add_fusion.2, s32[]{:T(128)S(6)} %select_n.19), kind=kOutput, calls=%fused_computation.3.clone.1 | convolution fusion | flops 4305452032 | bytes 6307844 | tf_op jit(solution)/shard_map/while/body/eval_jaxpr/dot_general | solution.py:34
  108.3 0.1 dynamic_update_slice.5
  108.4 0.6 dynamic_slice.12
  110.8 0.6 iota_add_fusion.2
  111.4 8.1 %select_reduce_fusion.2 = f32[1024]{0:T(1024)S(1)} fusion(bf16[2048,1024]{1,0:T(8,128)(2,1)} %get-tuple-element.93, f32[2048]{0:T(1024)S(1)} %get-tuple-element.94, s32[1024]{0:T(1024)S(1)} %iota_add_fusion.2, s32[]{:T(128)S(6)} %select_n.19), kind=kOutput, calls=%fused_computation.3.clone.1 | convolution fusion | flops 4305452032 | bytes 6307844 | tf_op jit(solution)/shard_map/while/body/eval_jaxpr/dot_general | solution.py:34
  119.6 0.1 dynamic_update_slice.5
  119.6 0.7 all_to_all.18
  120.4 4.5 %all-to-all-start.2 = ((f32[128,1,16]{2,1,0:T(1,128)}), f32[128,1,16]{2,1,0:T(1,128)S(1)}, u32[]{:S(2)}, u32[]{:S(2)}) async-start(f32[128,1,16]{2,1,0:T(1,128)} %bitcast.7), calls=%async_computation.2 | async-start | bytes 131072 | tf_op jit(solution)/shard_map/all_to_all | solution.py:77
  124.8 9.9 %all-to-all-done.2 = f32[128,1,16]{2,1,0:T(1,128)S(1)} async-done(((f32[128,1,16]{2,1,0:T(1,128)}), f32[128,1,16]{2,1,0:T(1,128)S(1)}, u32[]{:S(2)}, u32[]{:S(2)}) %all-to-all-start.2) | async-done | bytes 8224 | tf_op jit(solution)/shard_map/all_to_all | solution.py:77
  134.7 0.5 broadcast.62
  135.2 0.8 reduce.7
  136.0 0.1 reshape.56
  136.1 10.5 %gather_fusion = f32[1024]{0:T(1024)} fusion(f32[2048]{0:T(1024)S(1)} %reshape.56, s32[1024]{0:T(1024)S(1)} %broadcast_clamp_fusion), kind=kCustom, calls=%fused_computation | custom fusion | bytes 12288 | tf_op jit(solution)/shard_map/gather | solution.py:80
  (8 shorter events, 0.0 us)
Async XLA Ops:
  10.4 23.3 %all-to-all-start.1 = ((bf16[128,1,16]{2,1,0:T(2,128)(2,1)}), bf16[128,1,16]{2,1,0:T(2,128)(2,1)S(1)}, u32[]{:S(2)}, u32[]{:S(2)}) async-start(bf16[128,1,16]{2,1,0:T(2,128)(2,1)} %all_to_all.20), calls=%async_computation.1 | async-start | bytes 131072 | tf_op jit(solution)/shard_map/all_to_all | solution.py:68
  33.7 63.3 %all-to-all-start = ((bf16[128,16,1024]{2,1,0:T(8,128)(2,1)}), bf16[128,16,1024]{2,1,0:T(8,128)(2,1)}, u32[]{:S(2)}, u32[]{:S(2)}) async-start(bf16[128,16,1024]{2,1,0:T(8,128)(2,1)} %bitcast.15), calls=%async_computation | async-start | bytes 8388608 | tf_op jit(solution)/shard_map/all_to_all | solution.py:61
  120.4 14.4 %all-to-all-start.2 = ((f32[128,1,16]{2,1,0:T(1,128)}), f32[128,1,16]{2,1,0:T(1,128)S(1)}, u32[]{:S(2)}, u32[]{:S(2)}) async-start(f32[128,1,16]{2,1,0:T(1,128)} %bitcast.7), calls=%async_computation.2 | async-start | bytes 131072 | tf_op jit(solution)/shard_map/all_to_all | solution.py:77
where the time goes:
time: 147 us
  waiting for transfers between devices  62.7 us (43%)
  starting transfers between devices  26.2 us (18%)
  local copies, waits for them, and re-layouts  21.5 us (15%)
  matrix products  17.6 us (12%)
  other arithmetic  14.8 us (10%)
  loops' own time  3.78 us (3%)
    all_to_all x1, waiting for transfers between devices, shards(): lax.all_to_all(packed.reshape(devices, capacity, width), ('pool', 'blk'),...  52.8 us
    dot_general x2, matrix products, one_block(): lax.dot_general(queries, members, (((1,), (1,)), ((), ())), preferred_ele...  16.2 us
    all_to_all x1, starting transfers between devices, shards(): lax.all_to_all(present.reshape(devices, capacity), ('pool', 'blk'), split...  11.5 us
    gather x1, local copies, waits for them, and re-layouts, shards(): return back.reshape(total)[slot]  10.5 us
    all_to_all x1, starting transfers between devices, shards(): lax.all_to_all(packed.reshape(devices, capacity, width), ('pool', 'blk'),...  10.2 us
    all_to_all x1, waiting for transfers between devices, shards(): lax.all_to_all(dens.reshape(devices, capacity), ('pool', 'blk'), split_ax...  9.88 us
    scatter x1, other arithmetic, shards(): packed = jnp.zeros((total, width), jnp.bfloat16).at[slot].set(unit)  9.26 us
    scatter x1, local copies, waits for them, and re-layouts, shards(): jnp.zeros((total,), jnp.bfloat16).at[slot]  7.59 us
  transfers between devices with their start and end apart: 3, of which 2 were waited for; matrix products, arithmetic and copies ran while one was open for 8% of the time, Pallas kernels for 0%

commit v1 on v0

v1 whole, which is shorter than its diff:
```python
import jax
import jax.numpy as jnp
from jax import lax
from jax.experimental import pallas as pl
from jax.experimental.pallas import tpu as pltpu
from jax.sharding import PartitionSpec as P

EPSILON = 1e-06
SCALE = 50.0 * 1.4426950408889634
MESH = pl.DeviceIdType.MESH
ROWS = 1024
WIDTH = 1024
DEVICES = 128
CAP = 16
SLOTS = DEVICES * CAP
CHUNK = 256
CHUNKS = SLOTS // CHUNK
PER_CHUNK = CHUNK // CAP
STEP = 27
EMPTY = 1.25
NT = (((1,), (1,)), ((), ()))


def offset_of(k):
    v = ((k // 2) * STEP) % 64
    return v // 16, (v // 4) % 4, v % 4, k % 2


def place():
    pool = lax.axis_index("pool")
    return pool // 8, lax.axis_index("blk"), (pool // 2) % 4, pool % 2


def target(me, k):
    a, b, d, f = offset_of(k)
    x, y, z, c = (me[0] + a) % 4, (me[1] + b) % 4, (me[2] + d) % 4, (me[3] + f) % 2
    return x, y, z, c


def device_id(x, y, z, c):
    return ((x * 4 + z) * 2 + c, y)


def cluster_of(x, y, z, c):
    return (y * 2 + c) * 16 + x * 4 + z


def split3(v):
    hi = v.astype(jnp.bfloat16)
    rest = v - hi.astype(jnp.float32)
    mid = rest.astype(jnp.bfloat16)
    lo = (rest - mid.astype(jnp.float32)).astype(jnp.bfloat16)
    return hi, mid, lo


def kernel(
    emb_ref, ids_ref, out_ref,
    unit, send, recv, flags, acc, ret0, ret1, ret2, ret3,
    send_sem, recv_sem, s1_sem, r1_sem, s2_sem, r2_sem,
):
    me = place()
    x, y, z, c = me

    barrier = pltpu.get_barrier_semaphore()

    def greet(k, _):
        pl.semaphore_signal(
            barrier, inc=1, device_id=device_id(*target(me, k)), device_id_type=MESH
        )
        return 0

    lax.fori_loop(1, DEVICES, greet, 0)

    for b in range(4):
        rows = pl.ds(b * 256, 256)
        e = emb_ref[rows, :]
        squares = jnp.sum(e * e, axis=1, keepdims=True)
        unit[rows, :] = (e * lax.rsqrt(squares + EPSILON)).astype(jnp.bfloat16)

    ids = ids_ref[...]
    cluster = lax.broadcasted_iota(jnp.int32, (DEVICES, ROWS), 0)
    onehot = jnp.where(cluster == ids, 1.0, 0.0)
    onehot16 = onehot.astype(jnp.bfloat16)
    upper = jnp.where(
        lax.broadcasted_iota(jnp.int32, (256, 256), 0)
        < lax.broadcasted_iota(jnp.int32, (256, 256), 1),
        1.0, 0.0,
    ).astype(jnp.bfloat16)
    carry = jnp.zeros((DEVICES, 1), jnp.float32)
    ranks = []
    for b in range(4):
        cols = slice(b * 256, (b + 1) * 256)
        before = jnp.dot(onehot16[:, cols], upper, preferred_element_type=jnp.float32) + carry
        ranks.append(jnp.sum(before * onehot[:, cols], axis=0, keepdims=True))
        carry = before[:, 255:256] + onehot[:, b * 256 + 255 : b * 256 + 256]
    rank = jnp.concatenate(ranks, axis=1).astype(jnp.int32)
    slot = ids * CAP + rank

    def pack(t):
        i = t * CHUNK + lax.broadcasted_iota(jnp.int32, (CHUNK, 128), 0)
        wanted = cluster_vec(me, i // CAP) * CAP + i % CAP
        pick = jnp.where(slot == wanted[:, 0:1], 1.0, 0.0)
        held = jnp.sum(pick, axis=1, keepdims=True)
        packed = jnp.dot(pick.astype(jnp.bfloat16), unit[...], preferred_element_type=jnp.float32)
        lane = lax.broadcasted_iota(jnp.int32, (CHUNK, 128), 1)
        first = packed[:, :128] + jnp.where(lane == 0, EMPTY * (1.0 - held), 0.0)
        return jnp.concatenate([first, packed[:, 128:]], axis=1).astype(jnp.bfloat16)

    def cluster_vec(me, k):
        return cluster_of(*target(me, k))

    def start(k, t):
        rows = pl.ds(pl.multiple_of(k * CAP, CAP), CAP)
        pltpu.make_async_remote_copy(
            src_ref=send.at[rows],
            dst_ref=recv.at[rows],
            send_sem=send_sem,
            recv_sem=recv_sem.at[t],
            device_id=device_id(*target(me, k)),
            device_id_type=MESH,
        ).start()

    for t in range(CHUNKS):
        chunk = pack(t)
        send[pl.ds(t * CHUNK, CHUNK), :] = chunk
        if t == 0:
            recv[pl.ds(0, CAP), :] = chunk[:CAP]
            pl.semaphore_wait(barrier, DEVICES - 1)
        lo = t * PER_CHUNK

        def go(k, _, t=t):
            start(k, t)
            return 0

        lax.fori_loop(max(lo, 1), lo + PER_CHUNK, go, 0)

    acc[...] = jnp.zeros_like(acc)

    def block(u, t, diagonal):
        keys = pl.ds(pl.multiple_of(u * CHUNK, CHUNK), CHUNK)
        queries = pl.ds(pl.multiple_of(t * CHUNK, CHUNK), CHUNK)
        s = lax.dot_general(recv[keys, :], recv[queries, :], NT, preferred_element_type=jnp.float32)
        keep = flags[keys, :]
        w = jnp.exp2(s * SCALE) * jnp.concatenate([keep, keep], axis=1)
        if diagonal:
            own = lax.broadcasted_iota(jnp.int32, w.shape, 0)
            other = lax.broadcasted_iota(jnp.int32, w.shape, 1)
            w = jnp.where(own == other, 0.0, w)
        acc[:, queries] += jnp.sum(w.reshape(CHUNK // 8, 8, CHUNK), axis=0)

    for t in range(CHUNKS):
        skip = CAP if t == 0 else 0
        landed = recv.at[pl.ds(t * CHUNK + skip, CHUNK - skip)]
        pltpu.make_async_copy(landed, landed, recv_sem.at[t]).wait()
        rows = pl.ds(t * CHUNK, CHUNK)
        head = recv[rows, :128].astype(jnp.float32)[:, 0:1]
        flags[rows, :] = jnp.broadcast_to(jnp.where(head < 1.125, 1.0, 0.0), (CHUNK, 128))
        block(t, t, True)

        def others(u, _, t=t):
            block(u, t, False)
            block(t, u, False)
            return 0

        if t:
            lax.fori_loop(0, t, others, 0)

    density = jnp.log(1.0 + jnp.sum(acc[...], axis=0, keepdims=True))

    i = lax.broadcasted_iota(jnp.int32, (DEVICES, SLOTS), 1) // CAP
    a, b, d, f = offset_of(i)
    sx, sy, sz, sc = (x - a + 4) % 4, (y - b + 4) % 4, (z - d + 4) % 4, (c + f) % 2
    source = (sx * 4 + sz) * 8 + sy * 2 + sc
    mine = lax.broadcasted_iota(jnp.int32, (DEVICES, SLOTS), 0) == source
    spread = jnp.where(
        lax.broadcasted_iota(jnp.int32, (SLOTS, 128), 0) % CAP
        == lax.broadcasted_iota(jnp.int32, (SLOTS, 128), 1),
        1.0, 0.0,
    ).astype(jnp.bfloat16)
    total = jnp.zeros((DEVICES, 128), jnp.float32)
    for part in split3(density):
        rows = jnp.where(mine, part.astype(jnp.float32), 0.0).astype(jnp.bfloat16)
        total = total + jnp.dot(rows, spread, preferred_element_type=jnp.float32)
    ret0[...] = total

    xz = x * 4 + z

    def stage1(j, _):
        to = (xz + j) % 16
        pltpu.make_async_remote_copy(
            src_ref=ret0.at[pl.ds(pl.multiple_of(to * 8, 8), 8)],
            dst_ref=ret1.at[pl.ds(pl.multiple_of(xz * 8, 8), 8)],
            send_sem=s1_sem,
            recv_sem=r1_sem,
            device_id=(to * 2 + c, y),
            device_id_type=MESH,
        ).start()
        return 0

    lax.fori_loop(1, 16, stage1, 0)
    own = pl.ds(pl.multiple_of(xz * 8, 8), 8)
    ret1[own, :] = ret0[own, :]
    came = ret1.at[pl.ds(0, 120)]
    pltpu.make_async_copy(came, came, r1_sem).wait()
    for j in range(8):
        ret2[pl.ds(j * 16, 16), :] = ret1[pl.ds(j, 16, stride=8), :]
    yc = y * 2 + c

    def stage2(j, _):
        to = (yc + j) % 8
        pltpu.make_async_remote_copy(
            src_ref=ret2.at[pl.ds(pl.multiple_of(to * 16, 16), 16)],
            dst_ref=ret3.at[pl.ds(pl.multiple_of(yc * 16, 16), 16)],
            send_sem=s2_sem,
            recv_sem=r2_sem,
            device_id=(xz * 2 + to % 2, to // 2),
            device_id_type=MESH,
        ).start()
        return 0

    lax.fori_loop(1, 8, stage2, 0)
    own = pl.ds(pl.multiple_of(yc * 16, 16), 16)
    ret3[own, :] = ret2[own, :]
    came = ret3.at[pl.ds(0, 112)]
    pltpu.make_async_copy(came, came, r2_sem).wait()

    back = jnp.transpose(ret3[...])[:CAP, :]
    found = jnp.zeros((CAP, ROWS), jnp.float32)
    for part in split3(back):
        found = found + jnp.dot(part, onehot16, preferred_element_type=jnp.float32)
    at = lax.broadcasted_iota(jnp.int32, (CAP, ROWS), 0) == rank
    out_ref[...] = jnp.sum(jnp.where(at, found, 0.0), axis=0, keepdims=True)

    gone = send.at[pl.ds(CAP, SLOTS - CAP)]
    pltpu.make_async_copy(gone, gone, send_sem).wait()
    gone = ret0.at[pl.ds(0, 120)]
    pltpu.make_async_copy(gone, gone, s1_sem).wait()
    gone = ret2.at[pl.ds(0, 112)]
    pltpu.make_async_copy(gone, gone, s2_sem).wait()


def shards(embeddings, cluster_ids):
    vmem = pl.BlockSpec(memory_space=pltpu.VMEM)
    density = pl.pallas_call(
        kernel,
        out_shape=jax.ShapeDtypeStruct((1, ROWS), jnp.float32),
        in_specs=[vmem, vmem],
        out_specs=vmem,
        scratch_shapes=[
            pltpu.VMEM((ROWS, WIDTH), jnp.bfloat16),
            pltpu.VMEM((SLOTS, WIDTH), jnp.bfloat16),
            pltpu.VMEM((SLOTS, WIDTH), jnp.bfloat16),
            pltpu.VMEM((SLOTS, 128), jnp.float32),
            pltpu.VMEM((8, SLOTS), jnp.float32),
            pltpu.VMEM((DEVICES, 128), jnp.float32),
            pltpu.VMEM((DEVICES, 128), jnp.float32),
            pltpu.VMEM((DEVICES, 128), jnp.float32),
            pltpu.VMEM((DEVICES, 128), jnp.float32),
            pltpu.SemaphoreType.DMA,
            pltpu.SemaphoreType.DMA((CHUNKS,)),
            pltpu.SemaphoreType.DMA,
            pltpu.SemaphoreType.DMA,
            pltpu.SemaphoreType.DMA,
            pltpu.SemaphoreType.DMA,
        ],
        compiler_params=pltpu.CompilerParams(
            collective_id=0, has_side_effects=True, vmem_limit_bytes=48 << 20
        ),
        name="density",
    )(embeddings, cluster_ids.reshape(1, ROWS))
    return density.reshape(ROWS)


def solution(mesh):
    placed = (P(("pool", "blk"), None), P(("pool", "blk"), None))
    return jax.shard_map(
        shards, mesh=mesh, in_specs=placed, out_specs=P(("pool", "blk")), check_vma=False
    )
```

time: 147 us -> 88.4 us (0.60)
  Pallas kernels: 0 us -> 84.8 us
  waiting for transfers between devices: 62.7 us -> 0 us
  starting transfers between devices: 26.2 us -> 0 us
  local copies, waits for them, and re-layouts: 21.5 us -> 3.47 us
  matrix products: 17.6 us -> 0 us
  other arithmetic: 14.8 us -> 0 us
  loops' own time: 3.78 us -> 0 us
    pallas_call x0 -> x1, Pallas kernels: none -> 84.8 us  [shards(): pl.pallas_call(kernel, out_shape=jax.ShapeDtypeStruct((1, ROWS), jnp.floa...]
    all_to_all x3 -> x0, waiting for transfers between devices: 62.7 us -> none  [the longest x1 52.8 us: shards(): lax.all_to_all(packed.reshape(devices, capacity, width), ('pool', 'blk'),...]
    all_to_all x3 -> x0, starting transfers between devices: 26.2 us -> none  [the longest x1 11.5 us: shards(): lax.all_to_all(present.reshape(devices, capacity), ('pool', 'blk'), split...]
    dot_general x3 -> x0, matrix products: 17.6 us -> none  [the longest x2 16.2 us: one_block(): lax.dot_general(queries, members, (((1,), (1,)), ((), ())), preferred_ele...]
    gather x1 -> x0, local copies, waits for them, and re-layouts: 10.5 us -> none  [shards(): return back.reshape(total)[slot]]
    scatter x1 -> x0, other arithmetic: 9.26 us -> none  [shards(): packed = jnp.zeros((total, width), jnp.bfloat16).at[slot].set(unit)]
    scatter x1 -> x0, local copies, waits for them, and re-layouts: 7.59 us -> none  [shards(): jnp.zeros((total,), jnp.bfloat16).at[slot]]
    another operation x1 -> x0, loops' own time: 3.78 us -> none  [cluster_density(): return lax.map(one_block, starts).reshape(count)]
  transfers between devices with their start and end apart: 3 -> 0, of which waited for: 2 -> 0; matrix products, arithmetic and copies ran while one was open for 8% -> 0% of each run, Pallas kernels for 0% -> 0%
where the time goes in v1:
time: 88.4 us; the launch traced here: 88.3 us
  Pallas kernels  84.8 us (96%)
  local copies, waits for them, and re-layouts  3.47 us (4%)
    pallas_call x1, Pallas kernels, shards(): pl.pallas_call(kernel, out_shape=jax.ShapeDtypeStruct((1, ROWS), jnp.floa...  84.8 us
    unnamed x5, local copies, waits for them, and re-layouts  3.47 us

profile of v1, /device:TPU:1, one launch (start us, length us, event | category | flops | bytes accessed | tf_op | source)
XLA Modules:
  0.0 88.3 jit_solution(7605375106274298137)
XLA Ops:
  0.0 0.0 copy-start
  0.0 2.2 %copy-done = f32[1024,1024]{1,0:T(8,128)S(1)} copy-done((f32[1024,1024]{1,0:T(8,128)S(1)}, f32[1024,1024]{1,0:T(8,128)}, u32[]{:S(2)}) %copy-start) | copy-done | bytes 4194328
  2.2 0.0 copy-start.1
  2.2 0.7 copy-done.1
  2.9 84.8 %density.1 = f32[1,1024]{1,0:T(1,128)S(1)} custom-call(f32[1024,1024]{1,0:T(8,128)S(1)} %copy-done, s32[1,1024]{1,0:T(1,128)S(1)} %bitcast.3), custom_call_target="tpu_custom_call" | custom-call | tf_op jit(solution)/shard_map/density/pallas_call | solution.py:244
  87.7 0.6 copy.4
Async XLA Ops:
  0.0 2.2 %copy-start = (f32[1024,1024]{1,0:T(8,128)S(1)}, f32[1024,1024]{1,0:T(8,128)}, u32[]{:S(2)}) copy-start(f32[1024,1024]{1,0:T(8,128)} %emb_ref.1) | copy-start | bytes 12582916
  2.2 0.7 copy-start.1

commit v2 on v0

v2 whole, which is shorter than its diff:
```python
import jax
import jax.numpy as jnp
from jax import lax
from jax.experimental import pallas as pl
from jax.experimental.pallas import tpu as pltpu
from jax.sharding import PartitionSpec as P

EPSILON = 1e-06
SCALE = 50.0 * 1.4426950408889634
MESH = pl.DeviceIdType.MESH
ROWS = 1024
WIDTH = 1024
CAP = 16
CHIPS = 64
SLOTS = 2 * CHIPS * CAP
CHUNK = 256
CHUNKS = SLOTS // CHUNK
EMPTY = 1.25
NT = (((1,), (1,)), ((), ()))


def opposite(o):
    return tuple(-v % 4 for v in o)


def hops(o):
    return sum(min(v, 4 - v) for v in o)


def far_first():
    every = [(a, b, d) for a in range(4) for b in range(4) for d in range(4)]
    every.sort(key=lambda o: (-hops(o), o))
    pairs, singles = [], []
    for o in every:
        for turn in (o, o[2:] + o[:2], o[1:] + o[:1]):
            both = [turn, opposite(turn)]
            if both[0] == both[1]:
                if turn not in singles:
                    singles.append(turn)
            elif both not in pairs and both[::-1] not in pairs:
                pairs.append(both)
    order = []
    for t in range(8):
        count = 2 if t in (0, 1, 5, 7) else 0
        for both in pairs[: 4 - count // 2]:
            order += both
        pairs = pairs[4 - count // 2 :]
        at = len(order) - 8 + count if t < 7 else len(order)
        order[at:at] = singles[:count]
        singles = singles[count:]
    return order


ORDER = far_first()
BACK = [ORDER.index(opposite(o)) for o in ORDER]
GROUPS = [(t * CHUNK, CHUNK) for t in range(CHUNKS - 1)] + [
    (SLOTS - CHUNK, CHUNK // 2),
    (SLOTS - CHUNK // 2, CHUNK // 2),
]


def slot_of(j, f):
    return (j // 8) * CHUNK + f * (CHUNK // 2) + (j % 8) * CAP


def row_of(j):
    return (j // 8) * 8 + -j % 8


def split3(v):
    hi = v.astype(jnp.bfloat16)
    rest = v - hi.astype(jnp.float32)
    mid = rest.astype(jnp.bfloat16)
    lo = (rest - mid.astype(jnp.float32)).astype(jnp.bfloat16)
    return hi, mid, lo


def kernel(
    emb_hbm, ids_hbm, out_ref,
    emb, ids_ref, unit, send, recv, flags, acc, acc_rows, ret, sib, both, back,
    load_sem, ids_sem, send_sem, recv_sem, sib_send, sib_recv, back_send, back_recv,
):
    pool = lax.axis_index("pool")
    y = lax.axis_index("blk")
    x, z, c = lax.div(pool, 8), lax.rem(lax.div(pool, 2), 4), lax.rem(pool, 2)

    loads = []
    ids_copy = pltpu.make_async_copy(ids_hbm, ids_ref, ids_sem)
    ids_copy.start()
    for b in range(4):
        rows = pl.ds(b * 256, 256)
        copy = pltpu.make_async_copy(emb_hbm.at[rows], emb.at[rows], load_sem.at[b])
        copy.start()
        loads.append(copy)

    xs = [lax.rem(x + a, 4) for a in range(4)]
    ys = [lax.rem(y + a, 4) for a in range(4)]
    zs = [lax.rem(z + a, 4) for a in range(4)]
    cs = [c, 1 - c]
    px = [v * 8 for v in xs]
    pzc = [[zs[d] * 2 + cs[f] for f in range(2)] for d in range(4)]

    def device(j, f):
        a, b, d = ORDER[j]
        return (px[a] + pzc[d][f], ys[b])

    def chip(j):
        a, b, d = ORDER[j]
        return xs[a] * 16 + ys[b] * 4 + zs[d]

    barrier = pltpu.get_barrier_semaphore()
    for j in range(CHIPS):
        for f in range(2):
            if j < CHIPS - 1 or f:
                pl.semaphore_signal(
                    barrier, inc=1, device_id=device(j, f), device_id_type=MESH
                )

    ids_copy.wait()
    ids = ids_ref[...]
    cluster = lax.broadcasted_iota(jnp.int32, (128, ROWS), 0)
    onehot = jnp.where(cluster == ids, 1.0, 0.0)
    onehot16 = onehot.astype(jnp.bfloat16)
    upper = jnp.where(
        lax.broadcasted_iota(jnp.int32, (256, 256), 0)
        < lax.broadcasted_iota(jnp.int32, (256, 256), 1),
        1.0, 0.0,
    ).astype(jnp.bfloat16)
    carry = jnp.zeros((128, 1), jnp.float32)
    ranks = []
    for b in range(4):
        cols = slice(b * 256, (b + 1) * 256)
        before = jnp.dot(onehot16[:, cols], upper, preferred_element_type=jnp.float32) + carry
        ranks.append(jnp.sum(before * onehot[:, cols], axis=0, keepdims=True))
        carry = before[:, 255:256] + onehot[:, b * 256 + 255 : b * 256 + 256]
    rank = jnp.concatenate(ranks, axis=1).astype(jnp.int32)
    slot = ids * CAP + rank - lax.broadcasted_iota(jnp.int32, (CAP, ROWS), 0)

    for b in range(4):
        loads[b].wait()
        rows = pl.ds(b * 256, 256)
        e = emb[rows, :]
        squares = jnp.sum(e * e, axis=1, keepdims=True)
        unit[rows, :] = (e * lax.rsqrt(squares + EPSILON)).astype(jnp.bfloat16)

    lane0 = lax.broadcasted_iota(jnp.int32, (CHUNK, 128), 1) == 0

    def pack(t):
        pick = jnp.concatenate(
            [
                jnp.where(slot == (chip(8 * t + j) * 2 + cs[f]) * CAP, 1.0, 0.0)
                for f in range(2)
                for j in range(8)
            ],
            axis=0,
        )
        held = jnp.sum(pick, axis=1, keepdims=True)
        packed = jnp.dot(pick.astype(jnp.bfloat16), unit[...], preferred_element_type=jnp.float32)
        first = packed[:, :128] + jnp.where(lane0, EMPTY * (1.0 - held), 0.0)
        return jnp.concatenate([first, packed[:, 128:]], axis=1).astype(jnp.bfloat16)

    def start(j, f):
        group = j // 8 + (f if j >= CHIPS - 8 else 0)
        pltpu.make_async_remote_copy(
            src_ref=send.at[pl.ds(slot_of(j, f), CAP)],
            dst_ref=recv.at[pl.ds(slot_of(BACK[j], f), CAP)],
            send_sem=send_sem,
            recv_sem=recv_sem.at[group],
            device_id=device(j, f),
            device_id_type=MESH,
        ).start()

    own = slot_of(CHIPS - 1, 0)
    for t in range(CHUNKS):
        chunk = pack(t)
        send[pl.ds(t * CHUNK, CHUNK), :] = chunk
        if t == 0:
            pl.semaphore_wait(barrier, 2 * CHIPS - 1)
        if t < CHUNKS - 1:
            for j in range(8 * t, 8 * t + 8):
                for f in range(2):
                    start(j, f)
        else:
            recv[pl.ds(own, CAP), :] = chunk[own - t * CHUNK : own - t * CHUNK + CAP]
            for f in range(2):
                for j in range(8 * t, 8 * t + 8):
                    if j < CHIPS - 1 or f:
                        start(j, f)

    acc[...] = jnp.zeros_like(acc)
    acc_rows[...] = jnp.zeros_like(acc_rows)
    pick0 = jnp.where(lax.broadcasted_iota(jnp.int32, (8, 128), 1) == 0, 1.0, 0.0).astype(jnp.bfloat16)

    for g, (q0, n) in enumerate(GROUPS):
        landed = recv.at[pl.ds(q0, n - CAP if q0 <= own < q0 + n else n)]
        pltpu.make_async_copy(landed, landed, recv_sem.at[g]).wait()
        head = recv[q0 : q0 + n, :128]
        mark = head.astype(jnp.float32)[:, 0:1]
        flags[q0 : q0 + n, :] = jnp.broadcast_to(jnp.where(mark < 1.125, 1.0, 0.0), (n, 128))
        marks = lax.dot_general(pick0, head, NT, preferred_element_type=jnp.float32)
        keep_q = jnp.where(marks[0:1, :] < 1.125, 1.0, 0.0)
        queries = recv[q0 : q0 + n, :]
        pieces = [(k, min(512, q0 - k)) for k in range(0, q0, 512)] + [(q0, n)]
        for k0, m in pieces:
            s = lax.dot_general(recv[k0 : k0 + m, :], queries, NT, preferred_element_type=jnp.float32)
            w = jnp.exp2(s * SCALE)
            if k0 == q0:
                w = jnp.where(
                    lax.broadcasted_iota(jnp.int32, (n, n), 0)
                    == lax.broadcasted_iota(jnp.int32, (n, n), 1),
                    0.0, w,
                )
            keep_k = flags[k0 : k0 + m, :]
            if n > 128:
                keep_k = jnp.concatenate([keep_k] * (n // 128), axis=1)
            acc[:, q0 : q0 + n] += jnp.sum((w * keep_k).reshape(m // 8, 8, n), axis=0)
            if k0 < q0:
                w = w * keep_q
                acc_rows[k0 : k0 + m, :] += sum(w[:, i : i + 128] for i in range(0, n, 128))

    rows = acc_rows[...]
    hi = rows.astype(jnp.bfloat16)
    mid = (rows - hi.astype(jnp.float32)).astype(jnp.bfloat16)
    turned = lax.dot_general(
        jnp.ones((8, 256), jnp.bfloat16), jnp.concatenate([hi, mid], axis=1), NT,
        preferred_element_type=jnp.float32,
    )
    density = jnp.log(1.0 + jnp.sum(acc[...], axis=0, keepdims=True) + turned[0:1, :])
    for i in range(2 * CHUNKS):
        tile = jnp.broadcast_to(density[:, i * 128 : i * 128 + 128], (8, 128))
        ret[i // 2, i % 2] = pltpu.roll(tile, 0, 1, stride=CAP, stride_axis=0)

    exchange = pltpu.make_async_remote_copy(
        src_ref=ret.at[:, 1],
        dst_ref=sib,
        send_sem=sib_send,
        recv_sem=sib_recv,
        device_id=(pool + 1 - 2 * c, y),
        device_id_type=MESH,
    )
    exchange.start()
    exchange.wait()
    low = lax.broadcasted_iota(jnp.int32, (8, 128), 1) < CAP
    for i in range(CHUNKS):
        mine, other = ret[i, 0], sib[i]
        first = jnp.where(c == 0, mine, other)
        second = jnp.where(c == 0, other, mine)
        both[pl.ds(i * 8, 8), :] = jnp.where(low, first, pltpu.roll(second, CAP, 1))
    back[pl.ds(CHIPS - 1, 1), :] = both[pl.ds(row_of(CHIPS - 1), 1), :]
    for j in range(CHIPS - 1):
        pltpu.make_async_remote_copy(
            src_ref=both.at[pl.ds(row_of(j), 1)],
            dst_ref=back.at[pl.ds(BACK[j], 1)],
            send_sem=back_send,
            recv_sem=back_recv,
            device_id=device(j, 0),
            device_id_type=MESH,
        ).start()

    row = lax.broadcasted_iota(jnp.int32, (CHIPS, 1), 0)
    chips = jnp.zeros((CHIPS, 1), jnp.int32)
    for j in range(CHIPS):
        chips = jnp.where(row == j, chip(j), chips)
    at_chip = jnp.where(lax.div(ids, 2) == chips, 1.0, 0.0).astype(jnp.bfloat16)
    at_lane = lax.broadcasted_iota(jnp.int32, (2 * CAP, ROWS), 0) == lax.rem(ids, 2) * CAP + rank

    came = back.at[pl.ds(0, CHIPS - 1)]
    pltpu.make_async_copy(came, came, back_recv).wait()
    turned = jnp.transpose(back[...])[: 2 * CAP, :]
    found = jnp.zeros((2 * CAP, ROWS), jnp.float32)
    for part in split3(turned):
        found = found + jnp.dot(part, at_chip, preferred_element_type=jnp.float32)
    out_ref[...] = jnp.sum(jnp.where(at_lane, found, 0.0), axis=0, keepdims=True)

    gone = send.at[pl.ds(CAP, SLOTS - CAP)]
    pltpu.make_async_copy(gone, gone, send_sem).wait()
    pltpu.make_async_copy(came, came, back_send).wait()


def shards(embeddings, cluster_ids):
    anywhere = pl.BlockSpec(memory_space=pl.ANY)
    density = pl.pallas_call(
        kernel,
        out_shape=jax.ShapeDtypeStruct((1, ROWS), jnp.float32),
        in_specs=[anywhere, anywhere],
        out_specs=pl.BlockSpec(memory_space=pltpu.VMEM),
        scratch_shapes=[
            pltpu.VMEM((ROWS, WIDTH), jnp.float32),
            pltpu.VMEM((1, ROWS), jnp.int32),
            pltpu.VMEM((ROWS, WIDTH), jnp.bfloat16),
            pltpu.VMEM((SLOTS, WIDTH), jnp.bfloat16),
            pltpu.VMEM((SLOTS, WIDTH), jnp.bfloat16),
            pltpu.VMEM((SLOTS, 128), jnp.float32),
            pltpu.VMEM((8, SLOTS), jnp.float32),
            pltpu.VMEM((SLOTS, 128), jnp.float32),
            pltpu.VMEM((CHUNKS, 2, 8, 128), jnp.float32),
            pltpu.VMEM((CHUNKS, 8, 128), jnp.float32),
            pltpu.VMEM((CHIPS, 128), jnp.float32),
            pltpu.VMEM((CHIPS, 128), jnp.float32),
            pltpu.SemaphoreType.DMA((4,)),
            pltpu.SemaphoreType.DMA,
            pltpu.SemaphoreType.DMA,
            pltpu.SemaphoreType.DMA((len(GROUPS),)),
            pltpu.SemaphoreType.DMA,
            pltpu.SemaphoreType.DMA,
            pltpu.SemaphoreType.DMA,
            pltpu.SemaphoreType.DMA,
        ],
        compiler_params=pltpu.CompilerParams(
            collective_id=0, has_side_effects=True, vmem_limit_bytes=60 << 20
        ),
        name="density",
    )(embeddings, cluster_ids.reshape(1, ROWS))
    return density.reshape(ROWS)


def solution(mesh):
    placed = (P(("pool", "blk"), None), P(("pool", "blk"), None))
    return jax.shard_map(
        shards, mesh=mesh, in_specs=placed, out_specs=P(("pool", "blk")), check_vma=False
    )
```

time: 147 us -> 79.1 us (0.54)
  Pallas kernels: 0 us -> 77.7 us
  waiting for transfers between devices: 62.7 us -> 0 us
  starting transfers between devices: 26.2 us -> 0 us
  local copies, waits for them, and re-layouts: 21.5 us -> 1.28 us
  matrix products: 17.6 us -> 0 us
  other arithmetic: 14.8 us -> 0 us
  loops' own time: 3.78 us -> 0 us
    pallas_call x0 -> x1, Pallas kernels: none -> 77.7 us  [shards(): pl.pallas_call(kernel, out_shape=jax.ShapeDtypeStruct((1, ROWS), jnp.floa...]
    all_to_all x3 -> x0, waiting for transfers between devices: 62.7 us -> none  [the longest x1 52.8 us: shards(): lax.all_to_all(packed.reshape(devices, capacity, width), ('pool', 'blk'),...]
    all_to_all x3 -> x0, starting transfers between devices: 26.2 us -> none  [the longest x1 11.5 us: shards(): lax.all_to_all(present.reshape(devices, capacity), ('pool', 'blk'), split...]
    dot_general x3 -> x0, matrix products: 17.6 us -> none  [the longest x2 16.2 us: one_block(): lax.dot_general(queries, members, (((1,), (1,)), ((), ())), preferred_ele...]
    gather x1 -> x0, local copies, waits for them, and re-layouts: 10.5 us -> none  [shards(): return back.reshape(total)[slot]]
    scatter x1 -> x0, other arithmetic: 9.26 us -> none  [shards(): packed = jnp.zeros((total, width), jnp.bfloat16).at[slot].set(unit)]
    scatter x1 -> x0, local copies, waits for them, and re-layouts: 7.59 us -> none  [shards(): jnp.zeros((total,), jnp.bfloat16).at[slot]]
    another operation x1 -> x0, loops' own time: 3.78 us -> none  [cluster_density(): return lax.map(one_block, starts).reshape(count)]
  transfers between devices with their start and end apart: 3 -> 0, of which waited for: 2 -> 0; matrix products, arithmetic and copies ran while one was open for 8% -> 0% of each run, Pallas kernels for 0% -> 0%
where the time goes in v2:
time: 79.1 us; the launch traced here: 79 us
  Pallas kernels  77.7 us (98%)
  local copies, waits for them, and re-layouts  1.28 us (2%)
    pallas_call x1, Pallas kernels, shards(): pl.pallas_call(kernel, out_shape=jax.ShapeDtypeStruct((1, ROWS), jnp.floa...  77.7 us

profile of v2, /device:TPU:1, one launch (start us, length us, event | category | flops | bytes accessed | tf_op | source)
XLA Modules:
  0.0 79.0 jit_solution(16382158674552518240)
XLA Ops:
  0.0 77.7 %density.1 = f32[1,1024]{1,0:T(1,128)} custom-call(f32[1024,1024]{1,0:T(8,128)} %emb_hbm.1, s32[1,1024]{1,0:T(1,128)} %bitcast.3), custom_call_target="tpu_custom_call" | custom-call | tf_op jit(solution)/shard_map/density/pallas_call | solution.py:282
  77.7 1.3 %copy.4 = f32[1024]{0:T(1024)} copy(f32[1024]{0:T(1024)} %bitcast.2) | data formatting | bytes 8192

commit v3 on v2

--- a/solution.py
+++ b/solution.py
@@ -53,6 +53,7 @@
 
 ORDER = far_first()
 BACK = [ORDER.index(opposite(o)) for o in ORDER]
+TILES = [t for g in range(8) for t in ((g, 0), ((g + 4) % 8, 1))]
 GROUPS = [(t * CHUNK, CHUNK) for t in range(CHUNKS - 1)] + [
     (SLOTS - CHUNK, CHUNK // 2),
     (SLOTS - CHUNK // 2, CHUNK // 2),
@@ -60,7 +61,7 @@
 
 
 def slot_of(j, f):
-    return (j // 8) * CHUNK + f * (CHUNK // 2) + (j % 8) * CAP
+    return TILES.index((j // 8, f)) * 8 * CAP + (j % 8) * CAP
 
 
 def row_of(j):
@@ -148,8 +149,8 @@
     def pack(t):
         pick = jnp.concatenate(
             [
-                jnp.where(slot == (chip(8 * t + j) * 2 + cs[f]) * CAP, 1.0, 0.0)
-                for f in range(2)
+                jnp.where(slot == (chip(8 * g + j) * 2 + cs[f]) * CAP, 1.0, 0.0)
+                for g, f in TILES[2 * t : 2 * t + 2]
                 for j in range(8)
             ],
             axis=0,
@@ -159,10 +160,13 @@
         first = packed[:, :128] + jnp.where(lane0, EMPTY * (1.0 - held), 0.0)
         return jnp.concatenate([first, packed[:, 128:]], axis=1).astype(jnp.bfloat16)
 
+    own = slot_of(CHIPS - 1, 0)
+
     def start(j, f):
-        group = j // 8 + (f if j >= CHIPS - 8 else 0)
+        at = slot_of(j, f)
+        group = max(g for g, (q0, _) in enumerate(GROUPS) if q0 <= at)
         pltpu.make_async_remote_copy(
-            src_ref=send.at[pl.ds(slot_of(j, f), CAP)],
+            src_ref=send.at[pl.ds(at, CAP)],
             dst_ref=recv.at[pl.ds(slot_of(BACK[j], f), CAP)],
             send_sem=send_sem,
             recv_sem=recv_sem.at[group],
@@ -170,22 +174,17 @@
             device_id_type=MESH,
         ).start()
 
-    own = slot_of(CHIPS - 1, 0)
     for t in range(CHUNKS):
         chunk = pack(t)
         send[pl.ds(t * CHUNK, CHUNK), :] = chunk
         if t == 0:
             pl.semaphore_wait(barrier, 2 * CHIPS - 1)
-        if t < CHUNKS - 1:
-            for j in range(8 * t, 8 * t + 8):
-                for f in range(2):
-                    start(j, f)
-        else:
+        if t == own // CHUNK:
             recv[pl.ds(own, CAP), :] = chunk[own - t * CHUNK : own - t * CHUNK + CAP]
-            for f in range(2):
-                for j in range(8 * t, 8 * t + 8):
-                    if j < CHIPS - 1 or f:
-                        start(j, f)
+        for i in range(8):
+            for g, f in TILES[2 * t : 2 * t + 2]:
+                if 8 * g + i < CHIPS - 1 or f:
+                    start(8 * g + i, f)
 
     acc[...] = jnp.zeros_like(acc)
     acc_rows[...] = jnp.zeros_like(acc_rows)
@@ -228,10 +227,11 @@
     density = jnp.log(1.0 + jnp.sum(acc[...], axis=0, keepdims=True) + turned[0:1, :])
     for i in range(2 * CHUNKS):
         tile = jnp.broadcast_to(density[:, i * 128 : i * 128 + 128], (8, 128))
-        ret[i // 2, i % 2] = pltpu.roll(tile, 0, 1, stride=CAP, stride_axis=0)
+        g, f = TILES[i]
+        ret[f, g] = pltpu.roll(tile, 0, 1, stride=CAP, stride_axis=0)
 
     exchange = pltpu.make_async_remote_copy(
-        src_ref=ret.at[:, 1],
+        src_ref=ret.at[1],
         dst_ref=sib,
         send_sem=sib_send,
         recv_sem=sib_recv,
@@ -242,7 +242,7 @@
     exchange.wait()
     low = lax.broadcasted_iota(jnp.int32, (8, 128), 1) < CAP
     for i in range(CHUNKS):
-        mine, other = ret[i, 0], sib[i]
+        mine, other = ret[0, i], sib[i]
         first = jnp.where(c == 0, mine, other)
         second = jnp.where(c == 0, other, mine)
         both[pl.ds(i * 8, 8), :] = jnp.where(low, first, pltpu.roll(second, CAP, 1))
@@ -278,7 +278,7 @@
 
 
 def shards(embeddings, cluster_ids):
-    anywhere = pl.BlockSpec(memory_space=pl.ANY)
+    anywhere = pl.BlockSpec(memory_space=pltpu.HBM)
     density = pl.pallas_call(
         kernel,
         out_shape=jax.ShapeDtypeStruct((1, ROWS), jnp.float32),
@@ -293,7 +293,7 @@
             pltpu.VMEM((SLOTS, 128), jnp.float32),
             pltpu.VMEM((8, SLOTS), jnp.float32),
             pltpu.VMEM((SLOTS, 128), jnp.float32),
-            pltpu.VMEM((CHUNKS, 2, 8, 128), jnp.float32),
+            pltpu.VMEM((2, CHUNKS, 8, 128), jnp.float32),
             pltpu.VMEM((CHUNKS, 8, 128), jnp.float32),
             pltpu.VMEM((CHIPS, 128), jnp.float32),
             pltpu.VMEM((CHIPS, 128), jnp.float32),
@@ -307,7 +307,7 @@
             pltpu.SemaphoreType.DMA,
         ],
         compiler_params=pltpu.CompilerParams(
-            collective_id=0, has_side_effects=True, vmem_limit_bytes=60 << 20
+            collective_id=0, has_side_effects=True, vmem_limit_bytes=56 << 20
         ),
         name="density",
     )(embeddings, cluster_ids.reshape(1, ROWS))

time: 79.1 us -> 71.6 us (0.905)
  Pallas kernels: 77.7 us -> 70.2 us
    pallas_call x1, Pallas kernels: 77.7 us -> 70.2 us  [shards(): pl.pallas_call(kernel, out_shape=jax.ShapeDtypeStruct((1, ROWS), jnp.floa...]
where the time goes in v3:
time: 71.6 us; the launch traced here: 71.5 us
  Pallas kernels  70.2 us (98%)
  local copies, waits for them, and re-layouts  1.28 us (2%)
    pallas_call x1, Pallas kernels, shards(): pl.pallas_call(kernel, out_shape=jax.ShapeDtypeStruct((1, ROWS), jnp.floa...  70.2 us

profile of v3, /device:TPU:1, one launch (start us, length us, event | category | flops | bytes accessed | tf_op | source)
XLA Modules:
  0.0 71.5 jit_solution(9882391264144297250)
XLA Ops:
  0.0 70.2 %density.1 = f32[1,1024]{1,0:T(1,128)} custom-call(f32[1024,1024]{1,0:T(8,128)} %emb_hbm.1, s32[1,1024]{1,0:T(1,128)} %bitcast.3), custom_call_target="tpu_custom_call" | custom-call | tf_op jit(solution)/shard_map/density/pallas_call | solution.py:282
  70.2 1.3 %copy.4 = f32[1024]{0:T(1024)} copy(f32[1024]{0:T(1024)} %bitcast.2) | data formatting | bytes 8192

commit v4 on v3

--- a/solution.py
+++ b/solution.py
@@ -53,11 +53,8 @@
 
 ORDER = far_first()
 BACK = [ORDER.index(opposite(o)) for o in ORDER]
-TILES = [t for g in range(8) for t in ((g, 0), ((g + 4) % 8, 1))]
-GROUPS = [(t * CHUNK, CHUNK) for t in range(CHUNKS - 1)] + [
-    (SLOTS - CHUNK, CHUNK // 2),
-    (SLOTS - CHUNK // 2, CHUNK // 2),
-]
+TILES = [t for g in range(8) for t in (((g + 4) % 8, 1), (g, 0))]
+GROUPS = [(t * CHUNK, CHUNK) for t in range(CHUNKS)]
 
 
 def slot_of(j, f):
@@ -182,7 +179,7 @@
         if t == own // CHUNK:
             recv[pl.ds(own, CAP), :] = chunk[own - t * CHUNK : own - t * CHUNK + CAP]
         for i in range(8):
-            for g, f in TILES[2 * t : 2 * t + 2]:
+            for g, f in TILES[2 * t : 2 * t + 2][::-1]:
                 if 8 * g + i < CHIPS - 1 or f:
                     start(8 * g + i, f)
 

time: 71.6 us -> 70.7 us (0.987)
  Pallas kernels: 70.2 us -> 69.3 us
    pallas_call x1, Pallas kernels: 70.2 us -> 69.3 us  [shards(): pl.pallas_call(kernel, out_shape=jax.ShapeDtypeStruct((1, ROWS), jnp.floa...]
where the time goes in v4:
time: 70.7 us; the launch traced here: 70.5 us
  Pallas kernels  69.3 us (98%)
  local copies, waits for them, and re-layouts  1.28 us (2%)
    pallas_call x1, Pallas kernels, shards(): pl.pallas_call(kernel, out_shape=jax.ShapeDtypeStruct((1, ROWS), jnp.floa...  69.3 us

profile of v4, /device:TPU:1, one launch (start us, length us, event | category | flops | bytes accessed | tf_op | source)
XLA Modules:
  0.0 70.5 jit_solution(4656441485199909652)
XLA Ops:
  0.0 69.3 %density.1 = f32[1,1024]{1,0:T(1,128)} custom-call(f32[1024,1024]{1,0:T(8,128)} %emb_hbm.1, s32[1,1024]{1,0:T(1,128)} %bitcast.3), custom_call_target="tpu_custom_call" | custom-call | tf_op jit(solution)/shard_map/density/pallas_call | solution.py:279
  69.3 1.3 %copy.4 = f32[1024]{0:T(1024)} copy(f32[1024]{0:T(1024)} %bitcast.2) | data formatting | bytes 8192

commit v5 on v4

--- a/solution.py
+++ b/solution.py
@@ -304,7 +304,7 @@
             pltpu.SemaphoreType.DMA,
         ],
         compiler_params=pltpu.CompilerParams(
-            collective_id=0, has_side_effects=True, vmem_limit_bytes=56 << 20
+            collective_id=0, has_side_effects=True, vmem_limit_bytes=55228 << 10
         ),
         name="density",
     )(embeddings, cluster_ids.reshape(1, ROWS))

time: 70.7 us -> 69.4 us (0.982)
  no operation moved by 1% of the time
where the time goes in v5:
time: 69.4 us; the launch traced here: 69.3 us
  Pallas kernels  68.7 us (99%)
    pallas_call x1, Pallas kernels, shards(): pl.pallas_call(kernel, out_shape=jax.ShapeDtypeStruct((1, ROWS), jnp.floa...  68.7 us

profile of v5, /device:TPU:1, one launch (start us, length us, event | category | flops | bytes accessed | tf_op | source)
XLA Modules:
  0.0 69.3 jit_solution(1398519825939080604)
XLA Ops:
  0.0 68.7 %density.1 = f32[1,1024]{1,0:T(1,128)S(1)} custom-call(f32[1024,1024]{1,0:T(8,128)} %emb_hbm.1, s32[1,1024]{1,0:T(1,128)} %bitcast.3), custom_call_target="tpu_custom_call" | custom-call | tf_op jit(solution)/shard_map/density/pallas_call | solution.py:279
  68.7 0.6 copy.4

commit v6 on v5

--- a/solution.py
+++ b/solution.py
@@ -53,7 +53,8 @@
 
 ORDER = far_first()
 BACK = [ORDER.index(opposite(o)) for o in ORDER]
-TILES = [t for g in range(8) for t in (((g + 4) % 8, 1), (g, 0))]
+OTHER = (4, 5, 6, 7, 0, 1, 2, 3)
+TILES = [t for g in range(8) for t in ((OTHER[g], 1), (g, 0))]
 GROUPS = [(t * CHUNK, CHUNK) for t in range(CHUNKS)]
 
 
@@ -180,8 +181,9 @@
             recv[pl.ds(own, CAP), :] = chunk[own - t * CHUNK : own - t * CHUNK + CAP]
         for i in range(8):
             for g, f in TILES[2 * t : 2 * t + 2][::-1]:
-                if 8 * g + i < CHIPS - 1 or f:
-                    start(8 * g + i, f)
+                j = 8 * g + (i + 4 * f) % 8
+                if j < CHIPS - 1 or f:
+                    start(j, f)
 
     acc[...] = jnp.zeros_like(acc)
     acc_rows[...] = jnp.zeros_like(acc_rows)

time: 69.4 us -> 68.8 us (level)
  Pallas kernels: 68.7 us -> 68 us
where the time goes in v6:
time: 68.8 us; the launch traced here: 68.7 us
  Pallas kernels  68 us (99%)
    pallas_call x1, Pallas kernels, shards(): pl.pallas_call(kernel, out_shape=jax.ShapeDtypeStruct((1, ROWS), jnp.floa...  68 us

profile of v6, /device:TPU:1, one launch (start us, length us, event | category | flops | bytes accessed | tf_op | source)
XLA Modules:
  0.0 68.7 jit_solution(12130215016127597901)
XLA Ops:
  0.0 68.0 %density.1 = f32[1,1024]{1,0:T(1,128)S(1)} custom-call(f32[1024,1024]{1,0:T(8,128)} %emb_hbm.1, s32[1,1024]{1,0:T(1,128)} %bitcast.3), custom_call_target="tpu_custom_call" | custom-call | tf_op jit(solution)/shard_map/density/pallas_call | solution.py:281
  68.1 0.6 copy.4

commit v7 on v6

--- a/solution.py
+++ b/solution.py
@@ -246,7 +246,7 @@
         second = jnp.where(c == 0, other, mine)
         both[pl.ds(i * 8, 8), :] = jnp.where(low, first, pltpu.roll(second, CAP, 1))
     back[pl.ds(CHIPS - 1, 1), :] = both[pl.ds(row_of(CHIPS - 1), 1), :]
-    for j in range(CHIPS - 1):
+    for j in sorted(range(CHIPS - 1), key=lambda j: -hops(ORDER[j])):
         pltpu.make_async_remote_copy(
             src_ref=both.at[pl.ds(row_of(j), 1)],
             dst_ref=back.at[pl.ds(BACK[j], 1)],

time: 68.8 us -> 68.8 us (level)
  no operation moved by 1% of the time
where the time goes in v7:
time: 68.8 us; the launch traced here: 68.7 us
  Pallas kernels  68 us (99%)
    pallas_call x1, Pallas kernels, shards(): pl.pallas_call(kernel, out_shape=jax.ShapeDtypeStruct((1, ROWS), jnp.floa...  68 us

profile of v7, /device:TPU:1, one launch (start us, length us, event | category | flops | bytes accessed | tf_op | source)
XLA Modules:
  0.0 68.7 jit_solution(6779710720181955721)
XLA Ops:
  0.0 68.0 %density.1 = f32[1,1024]{1,0:T(1,128)S(1)} custom-call(f32[1024,1024]{1,0:T(8,128)} %emb_hbm.1, s32[1,1024]{1,0:T(1,128)} %bitcast.3), custom_call_target="tpu_custom_call" | custom-call | tf_op jit(solution)/shard_map/density/pallas_call | solution.py:281
  68.1 0.6 copy.4
